TPU v7x, 32 devices: a whole 2x2x4 slice. The times are simulated.
32 devices in a mesh: expert: 4 (over x, core), fsdp: 8 (over z, y).
Axes of the slice: x: 2, y: 2, z: 4, core: 2. Of those that a mesh axis runs over, the one named last changes fastest.
Arguments:
- tokens: bfloat16 [4096, 2048], P(('expert', 'fsdp')), may hold values from -6 to 6
- expert_ids: int32 [4096, 1], P(('expert', 'fsdp')), may hold values from 0 to 7; in each aligned block of 128 rows (0 to 127, 128 to 255, ...) at most 24 rows name the same one
- gate_weight: bfloat16 [8, 2048, 8192], P('expert', None, 'fsdp'), may hold values from -0.125 to 0.125
- up_weight: bfloat16 [8, 2048, 8192], P('expert', None, 'fsdp'), may hold values from -0.125 to 0.125
- hidden_grad: bfloat16 [8, 768, 8192], P('expert', None, 'fsdp'), may hold values from -0.1796875 to 0.1796875
Outputs:
- hidden: bfloat16 [8, 768, 8192], P('expert', None, 'fsdp')
- gate_grad: float32 [8, 2048, 8192], P('expert', None, 'fsdp')
- up_grad: float32 [8, 2048, 8192], P('expert', None, 'fsdp')
Inputs may be any that keep to these rules, and one draw needn't show every extreme that they name: `expert_ids`: within the tokens of one device (aligned blocks of 128 rows) no expert is named more than 24 times, a bound that some block reaches.
All inputs are finite; a program needn't handle non-finite values.
Results may differ from a plain program's by a relative error of at most 0.003.
Values may be sent and summed in bfloat16 or wider, within the bound.
A program may use at most 192 MiB of HBM per device.

v0:
```python
import jax
import jax.numpy as jnp
from jax import lax
from jax.sharding import PartitionSpec as P

CAP = 24


def make_fold(gate_part, up_part, grad_part, piece):
    groups, sources, count, model = piece.shape
    rows_flat = piece.reshape(groups, sources * count, model)
    gate = jnp.einsum("grd,gdf->grf", rows_flat, gate_part, preferred_element_type=jnp.float32)
    upval = jnp.einsum("grd,gdf->grf", rows_flat, up_part, preferred_element_type=jnp.float32)
    cotan = grad_part
    cotan = cotan.reshape(groups, sources * count, cotan.shape[3]).astype(jnp.float32)
    sigma = 1.0 / (1.0 + jnp.exp(-gate))
    active = gate * sigma
    hidden = (active * upval).astype(jnp.bfloat16)
    gate_delta = (cotan * upval * sigma * (1.0 + gate * (1.0 - sigma))).astype(jnp.bfloat16)
    up_delta = (cotan * active).astype(jnp.bfloat16)
    hidden_buf = hidden.reshape(groups, sources, count, hidden.shape[2])
    gate_sum = jnp.einsum("grd,grf->gdf", rows_flat, gate_delta, preferred_element_type=jnp.float32)
    up_sum = jnp.einsum("grd,grf->gdf", rows_flat, up_delta, preferred_element_type=jnp.float32)
    return (hidden_buf, gate_sum, up_sum)


def on_device(tokens, expert_ids, gate_weight, up_weight, hidden_grad):
    owners = lax.axis_size("expert")
    members = lax.axis_size("fsdp")
    per_owner = gate_weight.shape[0]
    model = gate_weight.shape[1]
    width = gate_weight.shape[2]
    route = expert_ids[:, 0]
    total_experts = per_owner * owners
    onehot = (route[:, None] == jnp.arange(total_experts, dtype=jnp.int32)[None, :]).astype(
        jnp.int32
    )
    rank = jnp.sum((jnp.cumsum(onehot, axis=0) - onehot) * onehot, axis=1)
    owner_of = route // per_owner
    within = route % per_owner
    target = within * (owners * CAP) + owner_of * CAP + rank
    send_rows = per_owner * owners * CAP
    placing = (jnp.arange(send_rows, dtype=jnp.int32)[:, None] == target[None, :]).astype(
        jnp.bfloat16
    )
    outgoing = jnp.dot(placing, tokens, preferred_element_type=jnp.float32).astype(jnp.bfloat16)
    outgoing = outgoing.reshape(per_owner, owners, CAP, model)
    slot_count = members * CAP
    grad_four = hidden_grad.reshape(per_owner, owners, slot_count, width)
    arrived = lax.all_to_all(outgoing, "expert", split_axis=1, concat_axis=1, tiled=True)
    hidden_buf, gate_sum, up_sum = make_fold(
        gate_weight, up_weight, grad_four, lax.all_gather(arrived, "fsdp", axis=2, tiled=True)
    )
    hidden = hidden_buf.reshape(per_owner, owners * slot_count, width)
    return (hidden, gate_sum, up_sum)


def solution(mesh):
    in_specs = (
        P(("expert", "fsdp"), None),
        P(("expert", "fsdp"), None),
        P("expert", None, "fsdp"),
        P("expert", None, "fsdp"),
        P("expert", None, "fsdp"),
    )
    out_specs = (P("expert", None, "fsdp"), P("expert", None, "fsdp"), P("expert", None, "fsdp"))
    return jax.shard_map(
        on_device, mesh=mesh, in_specs=in_specs, out_specs=out_specs, check_vma=False
    )
```

profile of v0, /device:TPU:0, one launch (start us, length us, event | category | flops | bytes accessed | tf_op | source)
XLA Modules:
  0.0 190.3 jit_solution(14605738642784010799)
XLA Ops:
  7.2 0.0 copy-start
  7.2 0.0 all-gather.2.cloned.1.call-start
  7.2 0.8 fusion.11
  8.0 0.2 reduce_window_sum.11
  8.2 0.8 select_reduce_fusion
  9.0 0.7 fusion.15
  9.7 0.0 copy-done
  9.7 0.4 convolution_convert_fusion
  10.1 0.1 copy.10
  10.2 15.8 %all_to_all.5 = bf16[2,4,24,2048]{3,2,0,1:T(8,128)(2,1)} all-to-all(bf16[2,4,24,2048]{3,2,0,1:T(8,128)(2,1)S(1)} %copy.10), channel_id=1, replica_groups=mesh['expert'=4,'fsdp'=8] {'expert'}, dimensions={1} | all-to-all | bytes 1572864 | tf_op jit(solution)/shard_map/all_to_all | solution.py:50
  25.9 0.0 all-gather.2.cloned.1.call-update
  25.9 100.0 %all-gather.2.cloned.1.call-done = bf16[2,4,192,2048]{3,2,0,1:T(8,128)(2,1)} async-done(((bf16[2,4,24,2048]{3,2,0,1:T(8,128)(2,1)}), bf16[2,4,192,2048]{3,2,0,1:T(8,128)(2,1)}) %all-gather.2.cloned.1.call-update) | async-done | bytes 6291472 | tf_op jit(solution)/shard_map/all_gather | solution.py:52
  125.9 0.0 slice-start
  125.9 3.5 %copy.11 = bf16[2,4,192,2048]{3,2,1,0:T(8,128)(2,1)S(1)} copy(bf16[2,4,192,2048]{3,2,0,1:T(8,128)(2,1)} %all-gather.2.cloned.1.call-done) | data formatting | bytes 12582912 | tf_op jit(solution)/shard_map/all_gather | solution.py:52
  129.5 0.0 copy-start.2
  129.5 0.0 slice-start.1
  129.5 13.0 %fusion.18 = f32[2,768,1024]{2,1,0:T(8,128)} fusion(bf16[2,768,2048]{2,1,0:T(8,128)(2,1)S(1)} %bitcast.11, bf16[2,2048,1024]{2,1,0:T(8,128)(2,1)} %param.7), kind=kOutput, calls=%fused_computation.28 | convolution fusion | flops 6442450944 | bytes 20971520 | tf_op jit(solution)/shard_map/grd,gdf->grf/dot_general | solution.py:12
  142.5 0.0 slice-done
  142.5 0.0 slice-done.1
  142.5 0.0 copy-start.3
  142.5 11.6 %multiply_convert_fusion = (bf16[2,768,1024]{2,1,0:T(8,128)(2,1)}, f32[2,768,1024]{2,1,0:T(8,128)}) fusion(f32[2,768,1024]{2,1,0:T(8,128)} %fusion.18, bf16[2,768,2048]{2,1,0:T(8,128)(2,1)S(1)} %bitcast.12, bf16[2,2048,1024]{2,1,0:T(8,128)(2,1)S(1)} %bitcast.19), kind=kOutput, calls=%fused_computation.6 | convolution fusion | flops 6451888128 | bytes 30408704 | tf_op jit(solution)/shard_map/grd,gdf->grf/dot_general | solution.py:13
  154.1 0.0 copy-done.2
  154.1 0.0 copy-done.3
  154.1 13.3 %fusion.5 = f32[2,2048,1024]{2,1,0:T(8,128)} fusion(bf16[2,768,2048]{2,1,0:T(8,128)(2,1)S(1)} %bitcast.13, bf16[2,768,1024]{2,1,0:T(8,128)(2,1)S(1)} %copy-done.3, f32[2,768,1024]{2,1,0:T(8,128)} %fusion.18), kind=kOutput, calls=%fused_computation.9 | convolution fusion | flops 6453460992 | bytes 32505856 | tf_op jit(solution)/shard_map/grd,grf->gdf/dot_general | solution.py:23
  167.5 0.0 copy-start.1
  167.5 15.9 %fusion.7 = f32[2,2048,1024]{2,1,0:T(8,128)} fusion(bf16[2,768,2048]{2,1,0:T(8,128)(2,1)} %bitcast.14, f32[2,768,1024]{2,1,0:T(8,128)} %get-tuple-element.4, bf16[2,768,1024]{2,1,0:T(8,128)(2,1)} %param.9, f32[2,768,1024]{2,1,0:T(8,128)} %fusion.18), kind=kOutput, calls=%fused_computation.10 | convolution fusion | flops 6459752448 | bytes 38797312 | tf_op jit(solution)/shard_map/grd,grf->gdf/dot_general | solution.py:22
  183.4 0.0 copy-done.1
  (1 shorter events, 0.0 us)
Async XLA Ops:
  7.2 2.5 %copy-start = (bf16[128,2048]{1,0:T(8,128)(2,1)S(1)}, bf16[128,2048]{1,0:T(8,128)(2,1)}, u32[]{:S(2)}) copy-start(bf16[128,2048]{1,0:T(8,128)(2,1)} %param.5) | copy-start | bytes 1572868
  7.2 118.7 %all-gather.2.cloned.1.call-start = ((), (), s32[]{:S(2)}) async-start(), calls=%async_computation.1 | async-start | bytes 7077888 | tf_op jit(solution)/shard_map/all_gather | solution.py:52
  125.9 16.6 %slice-start = ((s8[8388608]{0:T(1024)(128)(4,1)}), s8[4194304]{0:T(1024)(128)(4,1)S(1)}, s32[]{:S(2)}) async-start(s8[8388608]{0:T(1024)(128)(4,1)} %bitcast.18), calls=%async_computation.2 | async-start | bytes 8388608
  129.5 24.7 %copy-start.2 = (bf16[2,4,192,2048]{3,2,1,0:T(8,128)(2,1)}, bf16[2,4,192,2048]{3,2,1,0:T(8,128)(2,1)S(1)}, u32[]{:S(2)}) copy-start(bf16[2,4,192,2048]{3,2,1,0:T(8,128)(2,1)S(1)} %copy.11) | copy-start | bytes 18874372
  129.5 13.0 %slice-start.1 = ((s8[8388608]{0:T(1024)(128)(4,1)}), s8[4194304]{0:T(1024)(128)(4,1)S(1)}, s32[]{:S(2)}) async-start(s8[8388608]{0:T(1024)(128)(4,1)} %bitcast.18), calls=%async_computation.3 | async-start | bytes 8388608
  142.5 11.6 %copy-start.3 = (bf16[2,768,1024]{2,1,0:T(8,128)(2,1)S(1)}, bf16[2,768,1024]{2,1,0:T(8,128)(2,1)}, u32[]{:S(2)}) copy-start(bf16[2,768,1024]{2,1,0:T(8,128)(2,1)} %param.9) | copy-start | bytes 9437188
  167.5 15.9 %copy-start.1 = (bf16[128,2048]{1,0:T(8,128)(2,1)S(1)}, bf16[128,2048]{1,0:T(8,128)(2,1)}, u32[]{:S(2)}) copy-start(bf16[128,2048]{1,0:T(8,128)(2,1)} %param.5) | copy-start | bytes 1572868
Sparse Core Ops, SparseCore 0:
  26.1 99.8 all-gather.1
where the time goes:
time: 191 us; the launch traced here: 190 us
  waiting for transfers between devices  100 us (52%)
  matrix products  54.3 us (28%)
  blocking collectives  15.8 us (8%)
  between operations  14.1 us (7%)
  local copies, waits for them, and re-layouts  3.63 us (2%)
  other arithmetic  2.46 us (1%)
    all_gather x1, waiting for transfers between devices, on_device(): lax.all_gather(arrived, 'fsdp', axis=2, tiled=True)  100 us
    dot_general x1, matrix products, make_fold(): jnp.einsum('grd,grf->gdf', rows_flat, gate_delta, preferred_element_type=...  15.9 us
    all_to_all x1, blocking collectives, on_device(): lax.all_to_all(outgoing, 'expert', split_axis=1, concat_axis=1, tiled=True)  15.8 us
    dot_general x1, matrix products, make_fold(): jnp.einsum('grd,grf->gdf', rows_flat, up_delta, preferred_element_type=jn...  13.3 us
    dot_general x1, matrix products, make_fold(): jnp.einsum('grd,gdf->grf', rows_flat, gate_part, preferred_element_type=j...  13 us
    dot_general x1, matrix products, make_fold(): jnp.einsum('grd,gdf->grf', rows_flat, up_part, preferred_element_type=jnp...  11.6 us
  transfers between devices with their start and end apart: 1, of which 1 were waited for; matrix products, arithmetic and copies ran while one was open for 0% of the time, Pallas kernels for 0%

commit v1 on v0

v1 whole, which is shorter than its diff:
```python
import functools

import jax
import jax.numpy as jnp
from jax import lax
from jax.experimental import pallas as pl
from jax.experimental.pallas import tpu as pltpu
from jax.sharding import PartitionSpec as P

CAP = 24
MESH = pl.DeviceIdType.MESH
UP, DOWN, ACROSS = 0, 1, 2


def gather_kernel(levels, packed, rows, send_sem, first_sem, recv_sem, own_sem):
    e = lax.axis_index("expert")
    f = lax.axis_index("fsdp")
    pair, core = e // 2, e % 2
    z, y = f // 2, f % 2
    peers = [e, pair * 2 + (1 - core), (1 - pair) * 2 + core, (1 - pair) * 2 + (1 - core)]
    has_up, has_down = z < levels - 1, z > 0
    across = f + 1 - 2 * y

    barrier = pltpu.get_barrier_semaphore()

    def greet(device):
        pl.semaphore_signal(barrier, inc=1, device_id=device, device_id_type=MESH)

    for k in (1, 2, 3):
        greet((peers[k], f))
    greet((e, across))

    @pl.when(has_up)
    def _():
        greet((e, f + 2))

    @pl.when(has_down)
    def _():
        greet((e, f - 2))

    both = jnp.logical_and(has_up, has_down)

    @pl.when(both)
    def _():
        pl.semaphore_wait(barrier, 6)

    @pl.when(jnp.logical_not(both))
    def _():
        pl.semaphore_wait(barrier, 5)

    def copy(kind, fp, k, src=None):
        s = peers[k]
        target = {UP: f + 2, DOWN: f - 2, ACROSS: across}[kind]
        return pltpu.make_async_remote_copy(
            src_ref=rows.at[fp, s] if src is None else src,
            dst_ref=rows.at[fp, s],
            send_sem=send_sem.at[kind, fp, s],
            recv_sem=recv_sem.at[fp, s],
            device_id=(e, target),
            device_id_type=MESH,
        )

    def first(k):
        return pltpu.make_async_remote_copy(
            src_ref=packed.at[peers[k]],
            dst_ref=rows.at[f, e],
            send_sem=first_sem.at[k],
            recv_sem=recv_sem.at[f, e],
            device_id=(peers[k], f),
            device_id_type=MESH,
        )

    def arrived(fp, k):
        piece = rows.at[fp, peers[k]]
        pltpu.make_async_copy(piece, piece, recv_sem.at[fp, peers[k]]).wait()

    def along(fp, k, act, up=True, down=True, src=None):
        if up:

            @pl.when(has_up)
            def _():
                act(copy(UP, fp, k, src))

        if down:

            @pl.when(has_down)
            def _():
                act(copy(DOWN, fp, k, src))

    def start(c):
        c.start()

    def sent(c):
        c.wait_send()

    own = pltpu.make_async_copy(packed.at[e], rows.at[f, e], own_sem)
    own.start()
    for k in (2, 3, 1):
        first(k).start()
    copy(ACROSS, f, 0, packed.at[e]).start()
    along(f, 0, start, src=packed.at[e])
    for k in (1, 2, 3):
        arrived(f, k)
        along(f, k, start)
        copy(ACROSS, f, k).start()
    arrived(across, 0)
    along(across, 0, start)
    for d in range(1, levels):
        for k in (0, 1, 2, 3):

            @pl.when(z >= d)
            def _():
                fp = f - 2 * d
                arrived(fp, k)
                along(fp, k, start, down=False)
                if k > 0:
                    copy(ACROSS, fp, k).start()

            @pl.when(z + d < levels)
            def _():
                fp = f + 2 * d
                arrived(fp, k)
                along(fp, k, start, up=False)
                if k > 0:
                    copy(ACROSS, fp, k).start()

        @pl.when(z >= d)
        def _():
            arrived(across - 2 * d, 0)
            along(across - 2 * d, 0, start, down=False)

        @pl.when(z + d < levels)
        def _():
            arrived(across + 2 * d, 0)
            along(across + 2 * d, 0, start, up=False)

    for level in range(levels):
        for k in (1, 2, 3):
            arrived(level * 2 + 1 - y, k)

    own.wait()
    for k in (2, 3, 1):
        first(k).wait_send()
    copy(ACROSS, f, 0, packed.at[e]).wait_send()
    along(f, 0, sent, src=packed.at[e])
    for k in (1, 2, 3):
        along(f, k, sent)
        copy(ACROSS, f, k).wait_send()
    along(across, 0, sent)
    for d in range(1, levels):

        @pl.when(z >= d)
        def _():
            for k in (0, 1, 2, 3):
                along(f - 2 * d, k, sent, down=False)
                if k > 0:
                    copy(ACROSS, f - 2 * d, k).wait_send()
            along(across - 2 * d, 0, sent, down=False)

        @pl.when(z + d < levels)
        def _():
            for k in (0, 1, 2, 3):
                along(f + 2 * d, k, sent, up=False)
                if k > 0:
                    copy(ACROSS, f + 2 * d, k).wait_send()
            along(across + 2 * d, 0, sent, up=False)


def gather_rows(packed, members):
    owners, height, model = packed.shape
    return pl.pallas_call(
        functools.partial(gather_kernel, members // 2),
        out_shape=jax.ShapeDtypeStruct((members, owners, height, model), packed.dtype),
        in_specs=[pl.BlockSpec(memory_space=pl.ANY)],
        out_specs=pl.BlockSpec(memory_space=pl.ANY),
        scratch_shapes=[
            pltpu.SemaphoreType.DMA((3, members, owners)),
            pltpu.SemaphoreType.DMA((owners,)),
            pltpu.SemaphoreType.DMA((members, owners)),
            pltpu.SemaphoreType.DMA,
        ],
        compiler_params=pltpu.CompilerParams(collective_id=0, has_side_effects=True),
    )(packed)


def fold(rows, gate_part, up_part, grad_part):
    gate = jnp.einsum("grd,gdf->grf", rows, gate_part, preferred_element_type=jnp.float32)
    upval = jnp.einsum("grd,gdf->grf", rows, up_part, preferred_element_type=jnp.float32)
    cotan = grad_part.astype(jnp.float32)
    sigma = 1.0 / (1.0 + jnp.exp(-gate))
    active = gate * sigma
    hidden = (active * upval).astype(jnp.bfloat16)
    gate_delta = (cotan * upval * sigma * (1.0 + gate * (1.0 - sigma))).astype(jnp.bfloat16)
    up_delta = (cotan * active).astype(jnp.bfloat16)
    gate_sum = jnp.einsum("grd,grf->gdf", rows, gate_delta, preferred_element_type=jnp.float32)
    up_sum = jnp.einsum("grd,grf->gdf", rows, up_delta, preferred_element_type=jnp.float32)
    return hidden, gate_sum, up_sum


def on_device(tokens, expert_ids, gate_weight, up_weight, hidden_grad):
    owners = lax.axis_size("expert")
    members = lax.axis_size("fsdp")
    per_owner, model = gate_weight.shape[:2]
    route = expert_ids[:, 0]
    total_experts = per_owner * owners
    onehot = (route[:, None] == jnp.arange(total_experts, dtype=jnp.int32)[None, :]).astype(
        jnp.int32
    )
    rank = jnp.sum((jnp.cumsum(onehot, axis=0) - onehot) * onehot, axis=1)
    target = route * CAP + rank
    placing = (
        jnp.arange(total_experts * CAP, dtype=jnp.int32)[:, None] == target[None, :]
    ).astype(jnp.bfloat16)
    packed = jnp.dot(placing, tokens, preferred_element_type=jnp.float32).astype(jnp.bfloat16)
    rows = gather_rows(packed.reshape(owners, per_owner * CAP, model), members)
    rows = rows.reshape(members, owners, per_owner, CAP, model).transpose(2, 1, 0, 3, 4)
    rows = rows.reshape(per_owner, owners * members * CAP, model)
    return fold(rows, gate_weight, up_weight, hidden_grad)


def solution(mesh):
    in_specs = (
        P(("expert", "fsdp"), None),
        P(("expert", "fsdp"), None),
        P("expert", None, "fsdp"),
        P("expert", None, "fsdp"),
        P("expert", None, "fsdp"),
    )
    out_specs = (P("expert", None, "fsdp"), P("expert", None, "fsdp"), P("expert", None, "fsdp"))
    return jax.shard_map(
        on_device, mesh=mesh, in_specs=in_specs, out_specs=out_specs, check_vma=False
    )
```

time: 191 us -> 133 us (0.70)
  waiting for transfers between devices: 100 us -> 0 us
  Pallas kernels: 0 us -> 72.6 us
  blocking collectives: 15.8 us -> 0 us
  between operations: 14.1 us -> 0.74 us
    all_gather x1 -> x0, waiting for transfers between devices: 100 us -> none  [on_device(): lax.all_gather(arrived, 'fsdp', axis=2, tiled=True)]
    pallas_call x0 -> x1, Pallas kernels: none -> 72.6 us  [gather_rows(): pl.pallas_call(functools.partial(gather_kernel, members // 2), out_shape=...]
    all_to_all x1 -> x0, blocking collectives: 15.8 us -> none  [on_device(): lax.all_to_all(outgoing, 'expert', split_axis=1, concat_axis=1, tiled=True)]
    all_gather x1 -> x0, local copies, waits for them, and re-layouts: 3.53 us -> none  [on_device(): lax.all_gather(arrived, 'fsdp', axis=2, tiled=True)]
    reshape x1, local copies, waits for them, and re-layouts: 0.07 us -> 3.53 us  [on_device(): rows.reshape(members, owners, per_owner, CAP, model)]
  transfers between devices with their start and end apart: 1 -> 0, of which waited for: 1 -> 0; matrix products, arithmetic and copies ran while one was open for 0% -> 0% of each run, Pallas kernels for 0% -> 0%
where the time goes in v1:
time: 133 us
  Pallas kernels  72.6 us (55%)
  matrix products  53.4 us (40%)
  local copies, waits for them, and re-layouts  3.57 us (3%)
  other arithmetic  2.46 us (2%)
    pallas_call x1, Pallas kernels, gather_rows(): pl.pallas_call(functools.partial(gather_kernel, members // 2), out_shape=...  72.6 us
    dot_general x1, matrix products, fold(): jnp.einsum('grd,grf->gdf', rows, gate_delta, preferred_element_type=jnp.f...  15.9 us
    dot_general x1, matrix products, fold(): jnp.einsum('grd,grf->gdf', rows, up_delta, preferred_element_type=jnp.flo...  15.4 us
    dot_general x1, matrix products, fold(): jnp.einsum('grd,gdf->grf', rows, gate_part, preferred_element_type=jnp.fl...  11.4 us
    dot_general x1, matrix products, fold(): jnp.einsum('grd,gdf->grf', rows, up_part, preferred_element_type=jnp.floa...  9.54 us
    reshape x1, local copies, waits for them, and re-layouts, on_device(): rows.reshape(members, owners, per_owner, CAP, model)  3.53 us

profile of v1, /device:TPU:0, one launch (start us, length us, event | category | flops | bytes accessed | tf_op | source)
XLA Modules:
  0.0 132.8 jit_solution(286648088658925817)
XLA Ops:
  0.6 0.0 copy-start
  0.6 0.8 fusion.11
  1.4 0.2 reduce_window_sum.11
  1.6 0.8 select_reduce_fusion
  2.5 0.7 multiply_add_fusion
  3.1 0.0 copy-done
  3.1 1.2 convolution_convert_fusion
  4.4 72.6 %shard_map.76 = bf16[8,4,48,2048]{3,2,1,0:T(8,128)(2,1)} custom-call(bf16[4,48,2048]{2,1,0:T(8,128)(2,1)} %bitcast.19), custom_call_target="tpu_custom_call" | custom-call | tf_op jit(solution)/shard_map/pallas_call | solution.py:171
  76.9 0.0 slice-start
  77.0 3.5 %copy.11 = bf16[8,4,2,24,2048]{4,3,0,1,2:T(8,128)(2,1)S(1)} copy(bf16[8,4,2,24,2048]{4,3,2,1,0:T(8,128)(2,1)} %bitcast.14) | data formatting | bytes 12582912 | tf_op jit(solution)/shard_map/reshape | solution.py:216
  80.5 0.0 copy-start.2
  80.5 0.0 slice-start.1
  80.5 11.4 %fusion.15 = f32[2,768,1024]{2,1,0:T(8,128)S(1)} fusion(bf16[2,768,2048]{2,1,0:T(8,128)(2,1)S(1)} %bitcast.15, bf16[2,2048,1024]{2,1,0:T(8,128)(2,1)} %param.7), kind=kOutput, calls=%fused_computation.21 | convolution fusion | flops 6442450944 | bytes 20971520 | tf_op jit(solution)/shard_map/grd,gdf->grf/dot_general | solution.py:187
  91.9 0.0 copy-done.2
  91.9 0.0 slice-done
  91.9 0.0 slice-done.1
  91.9 0.0 copy-start.3
  92.0 9.5 %multiply_convert_fusion = (bf16[2,768,1024]{2,1,0:T(8,128)(2,1)}, f32[2,768,1024]{2,1,0:T(8,128)}) fusion(f32[2,768,1024]{2,1,0:T(8,128)S(1)} %fusion.15, bf16[2,768,2048]{2,1,0:T(8,128)(2,1)S(1)} %bitcast.16, bf16[2,2048,1024]{2,1,0:T(8,128)(2,1)S(1)} %bitcast.23), kind=kOutput, calls=%fused_computation.6 | convolution fusion | flops 6451888128 | bytes 30408704 | tf_op jit(solution)/shard_map/grd,gdf->grf/dot_general | solution.py:188
  101.5 0.0 copy-done.3
  101.5 15.9 %fusion.7 = f32[2,2048,1024]{2,1,0:T(8,128)} fusion(bf16[2,768,2048]{2,1,0:T(8,128)(2,1)} %bitcast.17, f32[2,768,1024]{2,1,0:T(8,128)} %get-tuple-element.4, bf16[2,768,1024]{2,1,0:T(8,128)(2,1)} %param.9, f32[2,768,1024]{2,1,0:T(8,128)} %copy-done.3), kind=kOutput, calls=%fused_computation.10 | convolution fusion | flops 6459752448 | bytes 38797312 | tf_op jit(solution)/shard_map/grd,grf->gdf/dot_general | solution.py:195
  117.4 0.0 copy-start.1
  117.4 15.4 %fusion.5 = f32[2,2048,1024]{2,1,0:T(8,128)} fusion(bf16[2,768,2048]{2,1,0:T(8,128)(2,1)} %bitcast.18, bf16[2,768,1024]{2,1,0:T(8,128)(2,1)} %param.9, f32[2,768,1024]{2,1,0:T(8,128)} %copy-done.3), kind=kOutput, calls=%fused_computation.9 | convolution fusion | flops 6453460992 | bytes 32505856 | tf_op jit(solution)/shard_map/grd,grf->gdf/dot_general | solution.py:196
  132.8 0.0 copy-done.1
  (1 shorter events, 0.0 us)
Async XLA Ops:
  0.6 2.5 %copy-start = (bf16[128,2048]{1,0:T(8,128)(2,1)S(1)}, bf16[128,2048]{1,0:T(8,128)(2,1)}, u32[]{:S(2)}) copy-start(bf16[128,2048]{1,0:T(8,128)(2,1)} %param.5) | copy-start | bytes 1572868
  76.9 15.0 %slice-start = ((s8[8388608]{0:T(1024)(128)(4,1)}), s8[4194304]{0:T(1024)(128)(4,1)S(1)}, s32[]{:S(2)}) async-start(s8[8388608]{0:T(1024)(128)(4,1)} %bitcast.22), calls=%async_computation | async-start | bytes 8388608
  80.5 11.4 %copy-start.2 = (bf16[8,4,2,24,2048]{4,3,0,1,2:T(8,128)(2,1)}, bf16[8,4,2,24,2048]{4,3,0,1,2:T(8,128)(2,1)S(1)}, u32[]{:S(2)}) copy-start(bf16[8,4,2,24,2048]{4,3,0,1,2:T(8,128)(2,1)S(1)} %copy.11) | copy-start | bytes 18874372
  80.5 11.4 %slice-start.1 = ((s8[8388608]{0:T(1024)(128)(4,1)}), s8[4194304]{0:T(1024)(128)(4,1)S(1)}, s32[]{:S(2)}) async-start(s8[8388608]{0:T(1024)(128)(4,1)} %bitcast.22), calls=%async_computation.1 | async-start | bytes 8388608
  91.9 9.6 %copy-start.3 = (f32[2,768,1024]{2,1,0:T(8,128)}, f32[2,768,1024]{2,1,0:T(8,128)S(1)}, u32[]{:S(2)}) copy-start(f32[2,768,1024]{2,1,0:T(8,128)S(1)} %fusion.15) | copy-start | bytes 18874372
  117.4 15.4 %copy-start.1 = (bf16[128,2048]{1,0:T(8,128)(2,1)S(1)}, bf16[128,2048]{1,0:T(8,128)(2,1)}, u32[]{:S(2)}) copy-start(bf16[128,2048]{1,0:T(8,128)(2,1)} %param.5) | copy-start | bytes 1572868

commit v2 on v1

--- a/solution.py
+++ b/solution.py
@@ -12,7 +12,37 @@
 UP, DOWN, ACROSS = 0, 1, 2
 
 
-def gather_kernel(levels, packed, rows, send_sem, first_sem, recv_sem, own_sem):
+def gather_kernel(
+    levels,
+    tile,
+    packed,
+    gate_hbm,
+    up_hbm,
+    cotan_hbm,
+    rows,
+    slots_out,
+    hidden_out,
+    gate_out,
+    up_out,
+    gate_w,
+    up_w,
+    raw,
+    cotan,
+    block,
+    hidden,
+    gate_delta,
+    up_delta,
+    send_sem,
+    first_sem,
+    recv_sem,
+    own_sem,
+    load_sem,
+    store_sem,
+):
+    weights = [
+        pltpu.make_async_copy(gate_hbm, gate_w, load_sem.at[0]),
+        pltpu.make_async_copy(up_hbm, up_w, load_sem.at[1]),
+    ]
     e = lax.axis_index("expert")
     f = lax.axis_index("fsdp")
     pair, core = e // 2, e % 2
@@ -93,37 +123,105 @@
     def sent(c):
         c.wait_send()
 
+    groups, owners, height, model = block.shape
+    width = gate_w.shape[2]
+
+    def stores(level):
+        places = pl.ds(pl.multiple_of(level * height, 16), height)
+        return [
+            pltpu.make_async_copy(v, h.at[:, :, places], store_sem.at[i])
+            for i, (v, h) in enumerate(
+                (
+                    (block, slots_out),
+                    (hidden, hidden_out),
+                    (gate_delta, gate_out),
+                    (up_delta, up_out),
+                )
+            )
+        ]
+
+    def fetch(level):
+        for k in (1, 2, 3):
+            arrived(level * 2 + 1 - y, k)
+        places = pl.ds(pl.multiple_of(level * height, 16), height)
+        loads = [
+            pltpu.make_async_copy(rows.at[pl.ds(level * 2, 2)], raw, load_sem.at[2]),
+            pltpu.make_async_copy(cotan_hbm.at[:, :, places], cotan, load_sem.at[3]),
+        ]
+        for c in loads:
+            c.start()
+        for c in loads:
+            c.wait()
+        for s in range(owners):
+            for n in range(0, model, 512):
+                low = raw[0, s, :, n : n + 512].astype(jnp.float32)
+                high = raw[1, s, :, n : n + 512].astype(jnp.float32)
+                for g in range(groups):
+                    part = slice(g * CAP, (g + 1) * CAP)
+                    both_parts = jnp.concatenate([low[part], high[part]], axis=0)
+                    block[g, s, :, n : n + 512] = both_parts.astype(block.dtype)
+
+    def multiply(level, g):
+        flat = block[g].reshape(owners * height, model)
+
+        @pl.loop(0, width // tile)
+        def _(n):
+            cols = pl.ds(pl.multiple_of(n * tile, tile), tile)
+            gate = jnp.dot(flat, gate_w[g, :, cols], preferred_element_type=jnp.float32)
+            upval = jnp.dot(flat, up_w[g, :, cols], preferred_element_type=jnp.float32)
+            cot = cotan[g, :, :, cols].reshape(owners * height, tile).astype(jnp.float32)
+            sigma = 1.0 / (1.0 + jnp.exp(-gate))
+            active = gate * sigma
+            slope = sigma * (1.0 + gate * (1.0 - sigma))
+
+            def put(ref, value):
+                value = value.astype(ref.dtype).reshape(owners, height, tile)
+                ref[g, :, :, cols] = value
+
+            put(hidden, active * upval)
+            put(gate_delta, cot * upval * slope)
+            put(up_delta, cot * active)
+
+    def flush(level):
+        for c in stores(level):
+            c.start()
+        for c in stores(level):
+            c.wait()
+
     own = pltpu.make_async_copy(packed.at[e], rows.at[f, e], own_sem)
     own.start()
     for k in (2, 3, 1):
         first(k).start()
     copy(ACROSS, f, 0, packed.at[e]).start()
     along(f, 0, start, src=packed.at[e])
+    for c in weights:
+        c.start()
     for k in (1, 2, 3):
         arrived(f, k)
         along(f, k, start)
         copy(ACROSS, f, k).start()
     arrived(across, 0)
     along(across, 0, start)
-    for d in range(1, levels):
-        for k in (0, 1, 2, 3):
-
-            @pl.when(z >= d)
-            def _():
-                fp = f - 2 * d
-                arrived(fp, k)
-                along(fp, k, start, down=False)
-                if k > 0:
-                    copy(ACROSS, fp, k).start()
-
-            @pl.when(z + d < levels)
-            def _():
-                fp = f + 2 * d
-                arrived(fp, k)
-                along(fp, k, start, up=False)
-                if k > 0:
-                    copy(ACROSS, fp, k).start()
-
+    own.wait()
+    for c in weights:
+        c.wait()
+
+    def pass_on(d, k):
+        @pl.when(z >= d)
+        def _():
+            arrived(f - 2 * d, k)
+            along(f - 2 * d, k, start, down=False)
+            if k > 0:
+                copy(ACROSS, f - 2 * d, k).start()
+
+        @pl.when(z + d < levels)
+        def _():
+            arrived(f + 2 * d, k)
+            along(f + 2 * d, k, start, up=False)
+            if k > 0:
+                copy(ACROSS, f + 2 * d, k).start()
+
+    def pass_across(d):
         @pl.when(z >= d)
         def _():
             arrived(across - 2 * d, 0)
@@ -134,11 +232,42 @@
             arrived(across + 2 * d, 0)
             along(across + 2 * d, 0, start, up=False)
 
-    for level in range(levels):
-        for k in (1, 2, 3):
-            arrived(level * 2 + 1 - y, k)
-
-    own.wait()
+    def work(d, between):
+        below, above = z >= d, z + d < levels
+        nearer = z + d - 2 * d * ((z - d + levels) // levels)
+        paired = jnp.logical_and(jnp.logical_and(below, above), d > 0)
+        for level, valid in ((nearer, jnp.logical_or(below, above)), (z + d, paired)):
+
+            @pl.when(valid)
+            def _():
+                fetch(level)
+
+            between()
+            for g in range(groups):
+
+                @pl.when(valid)
+                def _():
+                    multiply(level, g)
+
+                between()
+
+            @pl.when(valid)
+            def _():
+                flush(level)
+
+    @pl.loop(1, levels + 1)
+    def _(d):
+        pending = [functools.partial(pass_on, d, k) for k in range(4)]
+        pending.append(functools.partial(pass_across, d))
+
+        def between():
+            if pending:
+                pending.pop(0)()
+
+        between()
+        between()
+        work(d - 1, between)
+
     for k in (2, 3, 1):
         first(k).wait_send()
     copy(ACROSS, f, 0, packed.at[e]).wait_send()
@@ -166,35 +295,73 @@
             along(across + 2 * d, 0, sent, up=False)
 
 
-def gather_rows(packed, members):
+def gather_rows(packed, gate_part, up_part, grad_part, members):
     owners, height, model = packed.shape
+    groups, _, width = gate_part.shape
+    dtype = packed.dtype
+    spread = (groups, owners, members * CAP)
+    narrow = jax.ShapeDtypeStruct(spread + (width,), dtype)
+    pair = (groups, owners, 2 * CAP)
     return pl.pallas_call(
-        functools.partial(gather_kernel, members // 2),
-        out_shape=jax.ShapeDtypeStruct((members, owners, height, model), packed.dtype),
-        in_specs=[pl.BlockSpec(memory_space=pl.ANY)],
-        out_specs=pl.BlockSpec(memory_space=pl.ANY),
+        functools.partial(gather_kernel, members // 2, min(256, width)),
+        out_shape=(
+            jax.ShapeDtypeStruct((members, owners, height, model), dtype),
+            jax.ShapeDtypeStruct(spread + (model,), dtype),
+            narrow,
+            narrow,
+            narrow,
+        ),
+        in_specs=[pl.BlockSpec(memory_space=pl.ANY)] * 4,
+        out_specs=(pl.BlockSpec(memory_space=pl.ANY),) * 5,
         scratch_shapes=[
+            pltpu.VMEM((groups, model, width), dtype),
+            pltpu.VMEM((groups, model, width), dtype),
+            pltpu.VMEM((2, owners, height, model), dtype),
+            pltpu.VMEM(pair + (width,), dtype),
+            pltpu.VMEM(pair + (model,), dtype),
+            pltpu.VMEM(pair + (width,), dtype),
+            pltpu.VMEM(pair + (width,), dtype),
+            pltpu.VMEM(pair + (width,), dtype),
             pltpu.SemaphoreType.DMA((3, members, owners)),
             pltpu.SemaphoreType.DMA((owners,)),
             pltpu.SemaphoreType.DMA((members, owners)),
             pltpu.SemaphoreType.DMA,
+            pltpu.SemaphoreType.DMA((4,)),
+            pltpu.SemaphoreType.DMA((4,)),
         ],
-        compiler_params=pltpu.CompilerParams(collective_id=0, has_side_effects=True),
-    )(packed)
-
-
-def fold(rows, gate_part, up_part, grad_part):
-    gate = jnp.einsum("grd,gdf->grf", rows, gate_part, preferred_element_type=jnp.float32)
-    upval = jnp.einsum("grd,gdf->grf", rows, up_part, preferred_element_type=jnp.float32)
-    cotan = grad_part.astype(jnp.float32)
-    sigma = 1.0 / (1.0 + jnp.exp(-gate))
-    active = gate * sigma
-    hidden = (active * upval).astype(jnp.bfloat16)
-    gate_delta = (cotan * upval * sigma * (1.0 + gate * (1.0 - sigma))).astype(jnp.bfloat16)
-    up_delta = (cotan * active).astype(jnp.bfloat16)
-    gate_sum = jnp.einsum("grd,grf->gdf", rows, gate_delta, preferred_element_type=jnp.float32)
-    up_sum = jnp.einsum("grd,grf->gdf", rows, up_delta, preferred_element_type=jnp.float32)
-    return hidden, gate_sum, up_sum
+        compiler_params=pltpu.CompilerParams(
+            collective_id=0, has_side_effects=True, vmem_limit_bytes=48 * 1024 * 1024
+        ),
+    )(packed, gate_part, up_part, grad_part.reshape(spread + (width,)))
+
+
+def grad_kernel(rows_ref, gate_ref, up_ref, gate_out, up_out):
+    dims = (((0,), (0,)), ((), ()))
+    rows = rows_ref[...]
+    gate_out[...] = lax.dot_general(rows, gate_ref[...], dims, preferred_element_type=jnp.float32)
+    up_out[...] = lax.dot_general(rows, up_ref[...], dims, preferred_element_type=jnp.float32)
+
+
+def weight_grads(rows, gate_delta, up_delta):
+    groups, slots, model = rows.shape
+    width = gate_delta.shape[2]
+    tile, cut = min(512, model), min(1024, width)
+    delta = pl.BlockSpec((None, slots, cut), lambda g, n, m: (g, 0, n))
+    out = pl.BlockSpec((None, tile, cut), lambda g, n, m: (g, m, n))
+    shape = jax.ShapeDtypeStruct((groups, model, width), jnp.float32)
+    return pl.pallas_call(
+        grad_kernel,
+        grid=(groups, width // cut, model // tile),
+        out_shape=(shape, shape),
+        in_specs=[pl.BlockSpec((None, slots, tile), lambda g, n, m: (g, 0, m)), delta, delta],
+        out_specs=(out, out),
+        compiler_params=pltpu.CompilerParams(vmem_limit_bytes=48 * 1024 * 1024),
+        cost_estimate=pl.CostEstimate(
+            flops=4 * groups * slots * model * width,
+            bytes_accessed=2 * groups * slots * (model + 2 * width) + 8 * groups * model * width,
+            transcendentals=0,
+        ),
+    )(rows, gate_delta, up_delta)
 
 
 def on_device(tokens, expert_ids, gate_weight, up_weight, hidden_grad):
@@ -212,10 +379,16 @@
         jnp.arange(total_experts * CAP, dtype=jnp.int32)[:, None] == target[None, :]
     ).astype(jnp.bfloat16)
     packed = jnp.dot(placing, tokens, preferred_element_type=jnp.float32).astype(jnp.bfloat16)
-    rows = gather_rows(packed.reshape(owners, per_owner * CAP, model), members)
-    rows = rows.reshape(members, owners, per_owner, CAP, model).transpose(2, 1, 0, 3, 4)
-    rows = rows.reshape(per_owner, owners * members * CAP, model)
-    return fold(rows, gate_weight, up_weight, hidden_grad)
+    blocks = packed.reshape(owners, per_owner * CAP, model)
+    _, rows, hidden, gate_delta, up_delta = gather_rows(
+        blocks, gate_weight, up_weight, hidden_grad, members
+    )
+
+    def by_slot(x):
+        return x.reshape(per_owner, owners * members * CAP, x.shape[3])
+
+    gate_sum, up_sum = weight_grads(by_slot(rows), by_slot(gate_delta), by_slot(up_delta))
+    return by_slot(hidden), gate_sum, up_sum
 
 
 def solution(mesh):

time: 133 us -> 108 us (0.81)
  matrix products: 53.4 us -> 0.36 us
  Pallas kernels: 72.6 us -> 101 us
    dot_general x4 -> x0, matrix products: 52.2 us -> none  [the longest x1 15.9 us: fold(): jnp.einsum('grd,grf->gdf', rows, gate_delta, preferred_element_type=jnp.f...]
    pallas_call x1 -> x2, Pallas kernels: 72.6 us -> 101 us  [the longest x1 81.4 us: gather_rows(): pl.pallas_call(functools.partial(gather_kernel, members // 2, min(256, wi...]
    reshape x1 -> x0, local copies, waits for them, and re-layouts: 3.53 us -> none  [on_device(): rows.reshape(members, owners, per_owner, CAP, model)]
    unnamed x12 -> x7, local copies, waits for them, and re-layouts: 0.04 us -> 3.56 us
where the time goes in v2:
time: 108 us
  Pallas kernels  101 us (94%)
  local copies, waits for them, and re-layouts  3.56 us (3%)
  other arithmetic  2.46 us (2%)
    pallas_call x1, Pallas kernels, gather_rows(): pl.pallas_call(functools.partial(gather_kernel, members // 2, min(256, wi...  81.4 us
    pallas_call x1, Pallas kernels, weight_grads(): pl.pallas_call(grad_kernel, grid=(groups, width // cut, model // tile), o...  19.4 us
    unnamed x7, local copies, waits for them, and re-layouts  3.56 us

profile of v2, /device:TPU:0, one launch (start us, length us, event | category | flops | bytes accessed | tf_op | source)
XLA Modules:
  0.0 107.8 jit_solution(3654638402890030881)
XLA Ops:
  0.6 0.0 copy-start
  0.6 0.8 fusion
  1.4 0.2 reduce_window_sum.11
  1.6 0.8 select_reduce_fusion
  2.5 0.7 multiply_add_fusion
  3.1 0.0 copy-done
  3.1 0.4 convolution_convert_fusion
  3.5 81.4 %shard_map.76 = (bf16[8,4,48,2048]{3,2,1,0:T(8,128)(2,1)}, bf16[2,4,192,2048]{3,2,1,0:T(8,128)(2,1)}, bf16[2,4,192,1024]{3,2,1,0:T(8,128)(2,1)S(1)}, bf16[2,4,19...) custom-call(bf16[4,48,2048]{2,1,0:T(8,128)(2,1)S(1)} %bitcast.9, bf16[2,2048,1024]{2,1,0:T(8,128)(2,1)} %gate_hbm.1, ...), custom_call_target="tpu_custom_call" | custom-call | tf_op jit(solution)/shard_map/pallas_call | solution.py:305
  84.8 0.0 copy-start.2
  84.9 1.9 %copy-done.2 = bf16[2,4,192,1024]{3,2,1,0:T(8,128)(2,1)S(1)} copy-done((bf16[2,4,192,1024]{3,2,1,0:T(8,128)(2,1)S(1)}, bf16[2,4,192,1024]{3,2,1,0:T(8,128)(2,1)}, u32[]{:S(2)}) %copy-start.2) | copy-done | bytes 3145752
  86.7 0.0 copy-start.1
  86.7 19.4 %shard_map.77 = (f32[2,2048,1024]{2,1,0:T(8,128)}, f32[2,2048,1024]{2,1,0:T(8,128)}) custom-call(bf16[2,768,2048]{2,1,0:T(8,128)(2,1)} %bitcast.15, bf16[2,768,1024]{2,1,0:T(8,128)(2,1)S(1)} %bitcast.11, bf16[2,768,1024]{2,1,0:T(8,128)(2,1)} %bitcast.16), custom_call_target="tpu_custom_call" | custom-call | flops 12884901888 | bytes 46137344 | tf_op jit(solution)/shard_map/pallas_call | solution.py:352
  106.1 1.7 %copy.9 = bf16[2,768,1024]{2,1,0:T(8,128)(2,1)} copy(bf16[2,768,1024]{2,1,0:T(8,128)(2,1)S(1)} %bitcast.10) | data formatting | bytes 6291456
  107.8 0.0 copy-done.1
Async XLA Ops:
  0.6 2.5 %copy-start = (bf16[128,2048]{1,0:T(8,128)(2,1)S(1)}, bf16[128,2048]{1,0:T(8,128)(2,1)}, u32[]{:S(2)}) copy-start(bf16[128,2048]{1,0:T(8,128)(2,1)} %param.5) | copy-start | bytes 1572868
  84.8 1.9 %copy-start.2 = (bf16[2,4,192,1024]{3,2,1,0:T(8,128)(2,1)S(1)}, bf16[2,4,192,1024]{3,2,1,0:T(8,128)(2,1)}, u32[]{:S(2)}) copy-start(bf16[2,4,192,1024]{3,2,1,0:T(8,128)(2,1)} %get-tuple-element.11) | copy-start | bytes 9437188
  86.7 21.1 %copy-start.1 = (bf16[128,2048]{1,0:T(8,128)(2,1)S(1)}, bf16[128,2048]{1,0:T(8,128)(2,1)}, u32[]{:S(2)}) copy-start(bf16[128,2048]{1,0:T(8,128)(2,1)} %param.5) | copy-start | bytes 1572868

commit v3 on v2

--- a/solution.py
+++ b/solution.py
@@ -330,55 +330,78 @@
             pltpu.SemaphoreType.DMA((4,)),
         ],
         compiler_params=pltpu.CompilerParams(
-            collective_id=0, has_side_effects=True, vmem_limit_bytes=48 * 1024 * 1024
+            collective_id=0, has_side_effects=True, vmem_limit_bytes=60 * 1024 * 1024
         ),
     )(packed, gate_part, up_part, grad_part.reshape(spread + (width,)))
 
 
-def grad_kernel(rows_ref, gate_ref, up_ref, gate_out, up_out):
-    dims = (((0,), (0,)), ((), ()))
-    rows = rows_ref[...]
-    gate_out[...] = lax.dot_general(rows, gate_ref[...], dims, preferred_element_type=jnp.float32)
-    up_out[...] = lax.dot_general(rows, up_ref[...], dims, preferred_element_type=jnp.float32)
-
-
-def weight_grads(rows, gate_delta, up_delta):
+def grad_kernel(rows_ref, gate_ref, up_ref, hidden_ref, hidden_out, gate_out, up_out):
+    turned = rows_ref[...].T
+    gate_out[...] = jnp.dot(turned, gate_ref[...], preferred_element_type=jnp.float32)
+    up_out[...] = jnp.dot(turned, up_ref[...], preferred_element_type=jnp.float32)
+    hidden_out[...] = hidden_ref[...]
+
+
+def weight_grads(rows, gate_delta, up_delta, hidden):
     groups, slots, model = rows.shape
     width = gate_delta.shape[2]
-    tile, cut = min(512, model), min(1024, width)
-    delta = pl.BlockSpec((None, slots, cut), lambda g, n, m: (g, 0, n))
-    out = pl.BlockSpec((None, tile, cut), lambda g, n, m: (g, m, n))
+    tile = min(512, model)
+    steps = model // tile
+    delta = pl.BlockSpec((None, slots, width), lambda g, m: (g, 0, 0))
+    part = pl.BlockSpec((None, slots // steps, width), lambda g, m: (g, m, 0))
+    out = pl.BlockSpec((None, tile, width), lambda g, m: (g, m, 0))
     shape = jax.ShapeDtypeStruct((groups, model, width), jnp.float32)
     return pl.pallas_call(
         grad_kernel,
-        grid=(groups, width // cut, model // tile),
-        out_shape=(shape, shape),
-        in_specs=[pl.BlockSpec((None, slots, tile), lambda g, n, m: (g, 0, m)), delta, delta],
-        out_specs=(out, out),
-        compiler_params=pltpu.CompilerParams(vmem_limit_bytes=48 * 1024 * 1024),
+        grid=(groups, steps),
+        out_shape=(jax.ShapeDtypeStruct(hidden.shape, hidden.dtype), shape, shape),
+        in_specs=[
+            pl.BlockSpec((None, slots, tile), lambda g, m: (g, 0, m)),
+            delta,
+            delta,
+            part,
+        ],
+        out_specs=(part, out, out),
+        compiler_params=pltpu.CompilerParams(vmem_limit_bytes=60 * 1024 * 1024),
         cost_estimate=pl.CostEstimate(
             flops=4 * groups * slots * model * width,
-            bytes_accessed=2 * groups * slots * (model + 2 * width) + 8 * groups * model * width,
+            bytes_accessed=2 * groups * slots * (model + 4 * width) + 8 * groups * model * width,
             transcendentals=0,
         ),
-    )(rows, gate_delta, up_delta)
+    )(rows, gate_delta, up_delta, hidden)
+
+
+def pack_kernel(ids_ref, tokens_ref, packed_ref):
+    count = tokens_ref.shape[0]
+    slots = packed_ref.shape[0]
+    ids = ids_ref[...]
+    lanes = lax.broadcasted_iota(jnp.int32, (count, 128), 1)
+    onehot = jnp.where(ids == lanes, 1.0, 0.0)
+    earlier = lax.broadcasted_iota(jnp.int32, (count, count), 1)
+    later = lax.broadcasted_iota(jnp.int32, (count, count), 0)
+    lower = jnp.where(earlier < later, 1.0, 0.0).astype(jnp.bfloat16)
+    before = jnp.dot(lower, onehot.astype(jnp.bfloat16), preferred_element_type=jnp.float32)
+    rank = jnp.sum(before * onehot, axis=1, keepdims=True)
+    target = ids * CAP + rank.astype(jnp.int32)
+    places = lax.broadcasted_iota(jnp.int32, (count, slots), 1)
+    placing = jnp.where(places == target, 1.0, 0.0).T.astype(jnp.bfloat16)
+    packed = jnp.dot(placing, tokens_ref[...], preferred_element_type=jnp.float32)
+    packed_ref[...] = packed.astype(packed_ref.dtype)
+
+
+def pack(expert_ids, tokens, experts):
+    return pl.pallas_call(
+        pack_kernel,
+        out_shape=jax.ShapeDtypeStruct((experts * CAP, tokens.shape[1]), tokens.dtype),
+        compiler_params=pltpu.CompilerParams(vmem_limit_bytes=32 * 1024 * 1024),
+    )(expert_ids, tokens)
 
 
 def on_device(tokens, expert_ids, gate_weight, up_weight, hidden_grad):
     owners = lax.axis_size("expert")
     members = lax.axis_size("fsdp")
     per_owner, model = gate_weight.shape[:2]
-    route = expert_ids[:, 0]
-    total_experts = per_owner * owners
-    onehot = (route[:, None] == jnp.arange(total_experts, dtype=jnp.int32)[None, :]).astype(
-        jnp.int32
-    )
-    rank = jnp.sum((jnp.cumsum(onehot, axis=0) - onehot) * onehot, axis=1)
-    target = route * CAP + rank
-    placing = (
-        jnp.arange(total_experts * CAP, dtype=jnp.int32)[:, None] == target[None, :]
-    ).astype(jnp.bfloat16)
-    packed = jnp.dot(placing, tokens, preferred_element_type=jnp.float32).astype(jnp.bfloat16)
+    packed = pack(expert_ids, tokens, per_owner * owners)
     blocks = packed.reshape(owners, per_owner * CAP, model)
     _, rows, hidden, gate_delta, up_delta = gather_rows(
         blocks, gate_weight, up_weight, hidden_grad, members
@@ -387,8 +410,7 @@
     def by_slot(x):
         return x.reshape(per_owner, owners * members * CAP, x.shape[3])
 
-    gate_sum, up_sum = weight_grads(by_slot(rows), by_slot(gate_delta), by_slot(up_delta))
-    return by_slot(hidden), gate_sum, up_sum
+    return weight_grads(by_slot(rows), by_slot(gate_delta), by_slot(up_delta), by_slot(hidden))
 
 
 def solution(mesh):

time: 108 us -> 108 us (level)
  Pallas kernels: 101 us -> 104 us
  other arithmetic: 2.46 us -> 0 us
    pallas_call x1 -> x2, Pallas kernels: 19.4 us -> 22.4 us  [the longest x1 21.6 us: weight_grads(): pl.pallas_call(grad_kernel, grid=(groups, steps), out_shape=(jax.ShapeDty...]
    unnamed x7 -> x5, local copies, waits for them, and re-layouts: 3.56 us -> 2.67 us
where the time goes in v3:
time: 108 us
  Pallas kernels  104 us (96%)
  local copies, waits for them, and re-layouts  2.67 us (2%)
    pallas_call x1, Pallas kernels, gather_rows(): pl.pallas_call(functools.partial(gather_kernel, members // 2, min(256, wi...  81.8 us
    pallas_call x1, Pallas kernels, weight_grads(): pl.pallas_call(grad_kernel, grid=(groups, steps), out_shape=(jax.ShapeDty...  21.6 us
    unnamed x5, local copies, waits for them, and re-layouts  2.67 us

profile of v3, /device:TPU:0, one launch (start us, length us, event | category | flops | bytes accessed | tf_op | source)
XLA Modules:
  0.0 107.5 jit_solution(11203013131929021533)
XLA Ops:
  0.6 0.8 copy.8.ids_ref
  1.4 0.0 copy-start.1
  1.4 1.0 copy-done.1
  2.4 0.8 shard_map.76
  3.2 0.0 copy-start
  3.2 0.9 copy-done
  4.1 81.8 %shard_map.77 = (bf16[8,4,48,2048]{3,2,1,0:T(8,128)(2,1)}, bf16[2,4,192,2048]{3,2,1,0:T(8,128)(2,1)}, bf16[2,4,192,1024]{3,2,1,0:T(8,128)(2,1)}, bf16[2,4,192,10...) custom-call(bf16[4,48,2048]{2,1,0:T(8,128)(2,1)} %bitcast.6, bf16[2,2048,1024]{2,1,0:T(8,128)(2,1)} %gate_hbm.1, ...), custom_call_target="tpu_custom_call" | custom-call | tf_op jit(solution)/shard_map/pallas_call | solution.py:305
  85.9 21.6 %shard_map.78 = (bf16[2,768,1024]{2,1,0:T(8,128)(2,1)}, f32[2,2048,1024]{2,1,0:T(8,128)}, f32[2,2048,1024]{2,1,0:T(8,128)}) custom-call(bf16[2,768,2048]{2,1,0:T(8,128)(2,1)} %bitcast.8, bf16[2,768,1024]{2,1,0:T(8,128)(2,1)} %bitcast.10, bf16[2,768,1024]{2,1,0:T(8,128)(2,1)} %bitcast.11, bf16[2,768,1024]{2,1,0:T(8,128)(2,1)} %bitcast.9), custom_call_target="tpu_custom_call" | custom-call | flops 12884901888 | bytes 52428800 | tf_op jit(solution)/shard_map/pallas_call | solution.py:354
Async XLA Ops:
  1.4 1.0 copy-start.1
  3.2 0.9 copy-start
